TPU v7x, 32 devices: a whole 2x2x4 slice. The times are simulated.
32 devices in a mesh: gx: 4 (over z), gy: 2 (over core), gz: 4 (over y, x).
Axes of the slice: x: 2, y: 2, z: 4, core: 2. Of those that a mesh axis runs over, the one named last changes fastest.
Arguments:
- charge: float32 [32, 64, 512], P('gx', 'gy', 'gz'), may hold values from -60 to 60
- texture: float32 [32, 64, 512], P('gx', 'gy', 'gz'), may hold values from 0.5 to 2
- material_eps: float32 [6], replicated, may hold values from 1 to 12
- layer_material: int32 [512], P('gz'), may hold values from 0 to 5
- gate_volts: float32 [1000], replicated, may hold values from -1 to 1
- block_cond: float32 [4096, 128], P(('gx', 'gy', 'gz')), may hold values from 2 to 20
- block_gate: int32 [4096], P(('gx', 'gy', 'gz')), may hold values from 0 to 999
- block_dest: int32 [4096], P(('gx', 'gy', 'gz')), may hold values from 0 to 7, as said below
- block_column: int32 [4096], P(('gx', 'gy', 'gz')), may hold values from 0 to 255
- initial: float32 [32, 64, 512], P('gx', 'gy', 'gz'), may hold values from -2 to 2
Outputs:
- potential: float32 [32, 64, 512], P('gx', 'gy', 'gz')
- residual_norm: float32 [], replicated
Inputs may be any that keep to these rules, and one draw needn't show every extreme that they name: `block_dest`: among the blocks of one device no value appears more than 64 times; one value appears exactly 64 times among the blocks of every device.
All inputs are finite; a program needn't handle non-finite values.
Results may differ from a plain program's by a relative error of at most 0.00002.
Values sent between devices are 32-bit elements; how exact they have to be, the bound alone decides.
A program may use at most 64 MiB of HBM per device.

v0:
```python
import jax
import jax.numpy as jnp
from jax import lax
from jax.sharding import PartitionSpec as P

SWEEPS = 4


relaxation = 0.8


def with_halo(block, sides, width):
    for axis, dim in sides:
        count = lax.axis_size(axis)
        forward = [(i, i + 1) for i in range(count - 1)]
        backward = [(target, source) for source, target in forward]
        low = lax.ppermute(
            lax.slice_in_dim(block, block.shape[dim] - width, None, axis=dim), axis, forward
        )
        high = lax.ppermute(lax.slice_in_dim(block, 0, width, axis=dim), axis, backward)
        block = jnp.concatenate([low, block, high], axis=dim)
    return block


def shifted(padded):
    return [
        padded[:-2, 1:-1, 1:-1],
        padded[2:, 1:-1, 1:-1],
        padded[1:-1, :-2, 1:-1],
        padded[1:-1, 2:, 1:-1],
        padded[1:-1, 1:-1, :-2],
        padded[1:-1, 1:-1, 2:],
    ]


def face_coefficients(padded):
    centre = padded[1:-1, 1:-1, 1:-1]
    result = []
    for neighbour in shifted(padded):
        result.append(2.0 * centre * neighbour / (centre + neighbour))
    return result


def neighbour_sum(coefficients, padded):
    pieces = shifted(padded)
    total_sum = coefficients[0] * pieces[0]
    for index in range(1, 6):
        total_sum = total_sum + coefficients[index] * pieces[index]
    return total_sum


def with_rim(potential):
    return with_halo(potential, (("gx", 0), ("gy", 1), ("gz", 2)), 1)


def table_lookup(table, indices):
    labels = jnp.arange(table.shape[0], dtype=jnp.int32)
    matches = indices[:, None] == labels[None, :]
    return jnp.sum(jnp.where(matches, table[None, :], 0.0), axis=1)


def on_device(
    charge,
    texture,
    material_eps,
    layer_material,
    gate_volts,
    block_cond,
    block_gate,
    block_dest,
    block_column,
    initial,
):
    cells_x, cells_y, cells_z = charge.shape
    grid_x = lax.axis_size("gx")
    grid_y = lax.axis_size("gy")
    peer_count = grid_x * grid_y
    block_count = block_dest.shape[0]
    capacity = max(2, 4 * block_count // peer_count)
    slot_total = peer_count * capacity
    layer_eps = table_lookup(material_eps, layer_material)
    permittivity = texture * layer_eps[None, None, :]
    same_dest = block_dest[:, None] == block_dest[None, :]
    order = jnp.arange(block_count, dtype=jnp.int32)
    earlier = order[None, :] < order[:, None]
    slot_rank = jnp.sum((same_dest & earlier).astype(jnp.int32), axis=1)
    position = block_dest * capacity + slot_rank
    cond_buf = jnp.zeros((slot_total, cells_z), jnp.float32).at[position].set(block_cond)
    column_buf = jnp.zeros((slot_total,), jnp.int32).at[position].set(block_column)
    block_volts = table_lookup(gate_volts, block_gate)
    extra_buf = (
        jnp.zeros((slot_total, cells_z), jnp.float32)
        .at[position]
        .set(block_cond * block_volts[:, None])
    )
    cond_recv, extra_recv, column_recv = (
        lax.all_to_all(cond_buf, ("gx", "gy"), split_axis=0, concat_axis=0, tiled=True),
        lax.all_to_all(extra_buf, ("gx", "gy"), split_axis=0, concat_axis=0, tiled=True),
        lax.all_to_all(column_buf, ("gx", "gy"), split_axis=0, concat_axis=0, tiled=True),
    )
    empty = jnp.zeros((cells_x * cells_y, cells_z), jnp.float32)
    coupling = empty.at[column_recv].add(cond_recv).reshape(cells_x, cells_y, cells_z)
    injected = empty.at[column_recv].add(extra_recv).reshape(cells_x, cells_y, cells_z)
    forcing = charge + injected
    padded_eps = with_halo(permittivity, (("gx", 0), ("gy", 1), ("gz", 2)), 1)
    coefficients = face_coefficients(padded_eps)
    diagonal_sum = coefficients[0]
    for index in range(1, 6):
        diagonal_sum = diagonal_sum + coefficients[index]
    diagonal_sum = diagonal_sum + coupling
    potential = initial
    for sweep in range(SWEEPS):
        neighbours = neighbour_sum(coefficients, with_rim(potential))
        potential = (1.0 - relaxation) * potential + relaxation * (
            forcing + neighbours
        ) / diagonal_sum
    neighbours = neighbour_sum(coefficients, with_rim(potential))
    residual = forcing + neighbours - diagonal_sum * potential
    squared_total = lax.psum(jnp.sum(residual * residual), ("gx", "gy", "gz"))
    cell_count = cells_x * cells_y * cells_z * grid_x * grid_y * lax.axis_size("gz")
    residual_norm = jnp.sqrt(squared_total / cell_count)
    return (potential, residual_norm)


def solution(mesh):
    in_specs = (
        P("gx", "gy", "gz"),
        P("gx", "gy", "gz"),
        P(),
        P("gz"),
        P(),
        P(("gx", "gy", "gz"), None),
        P(("gx", "gy", "gz")),
        P(("gx", "gy", "gz")),
        P(("gx", "gy", "gz")),
        P("gx", "gy", "gz"),
    )
    out_specs = (P("gx", "gy", "gz"), P())
    return jax.shard_map(
        on_device, mesh=mesh, in_specs=in_specs, out_specs=out_specs, check_vma=False
    )
```

profile of v0, /device:TPU:0, one launch (start us, length us, event | category | flops | bytes accessed | tf_op | source)
XLA Modules:
  0.0 211.6 jit_solution(3969632704521227581)
XLA Ops:
  3.4 6.3 %all-to-all-start = ((s32[8,64,1]{1,2,0:T(1,128)}), s32[8,64,1]{1,2,0:T(1,128)S(1)}, u32[]{:S(2)}, u32[]{:S(2)}) async-start(s32[8,64,1]{1,2,0:T(1,128)} %bitcast), calls=%async_computation | async-start | bytes 8192 | tf_op jit(solution)/shard_map/all_to_all | solution.py:99
  11.9 4.6 %collective-permute-start.1 = (f32[1,32,128]{2,1,0:T(8,128)S(1)}, f32[1,32,128]{2,1,0:T(8,128)S(1)}, u32[]{:S(2)}, u32[]{:S(2)}) collective-permute-start(f32[1,32,128]{2,1,0:T(8,128)S(1)} %get-tuple-element.41), channel_id=1, source_target_pairs={{0,8},{8,16},{16,24},{1,9},{9,17},{17,25},{2,10},{10,18},{18,26},{... | collective-permute-start | bytes 49160 | tf_op jit(solution)/shard_map/ppermute | solution.py:17
  18.9 4.6 %collective-permute-start = (f32[1,32,128]{2,1,0:T(8,128)S(1)}, f32[1,32,128]{2,1,0:T(8,128)S(1)}, u32[]{:S(2)}, u32[]{:S(2)}) collective-permute-start(f32[1,32,128]{2,1,0:T(8,128)S(1)} %get-tuple-element.39), channel_id=1, source_target_pairs={{0,8},{8,16},{16,24},{1,9},{9,17},{17,25},{2,10},{10,18},{18,26},{... | collective-permute-start | bytes 49160 | tf_op jit(solution)/shard_map/ppermute | solution.py:17
  26.9 4.3 %all-to-all-start.1 = ((f32[8,64,128]{2,1,0:T(8,128)}), f32[8,64,128]{2,1,0:T(8,128)S(1)}, u32[]{:S(2)}, u32[]{:S(2)}) async-start(f32[8,64,128]{2,1,0:T(8,128)} %bitcast.2), calls=%async_computation.1 | async-start | bytes 524288 | tf_op jit(solution)/shard_map/all_to_all | solution.py:98
  32.5 2.4 %collective-permute-start.5 = (f32[10,1,128]{2,1,0:T(1,128)S(1)}, f32[10,1,128]{2,1,0:T(1,128)S(1)}, u32[]{:S(2)}, u32[]{:S(2)}) collective-permute-start(f32[10,1,128]{2,1,0:T(1,128)S(1)} %get-tuple-element.28), channel_id=1, source_target_pairs={{0,4},{1,5},{2,6},{3,7},{8,12},{9,13},{10,14},{11,15},{16,20},{17,... | collective-permute-start | bytes 15368 | tf_op jit(solution)/shard_map/ppermute | solution.py:17
  37.6 3.0 %collective-permute-start.4 = (f32[10,1,128]{2,1,0:T(1,128)S(1)}, f32[10,1,128]{2,1,0:T(1,128)S(1)}, u32[]{:S(2)}, u32[]{:S(2)}) collective-permute-start(f32[10,1,128]{2,1,0:T(1,128)S(1)} %get-tuple-element.27), channel_id=1, source_target_pairs={{0,4},{1,5},{2,6},{3,7},{8,12},{9,13},{10,14},{11,15},{16,20},{17,... | collective-permute-start | bytes 15368 | tf_op jit(solution)/shard_map/ppermute | solution.py:17
  40.8 3.4 %collective-permute-start.9 = (f32[10,34,1]{2,1,0:T(8,128)S(1)}, f32[10,34,1]{2,1,0:T(8,128)S(1)}, u32[]{:S(2)}, u32[]{:S(2)}) collective-permute-start(f32[10,34,1]{2,1,0:T(8,128)S(1)} %get-tuple-element.16), channel_id=1, source_target_pairs={{0,1},{1,2},{2,3},{4,5},{5,6},{6,7},{8,9},{9,10},{10,11},{12,13},{... | collective-permute-start | bytes 4088 | tf_op jit(solution)/shard_map/ppermute | solution.py:17
  45.6 4.8 %all-to-all-start.2 = ((f32[8,64,128]{2,1,0:T(8,128)}), f32[8,64,128]{2,1,0:T(8,128)S(1)}, u32[]{:S(2)}, u32[]{:S(2)}) async-start(f32[8,64,128]{2,1,0:T(8,128)} %bitcast.5), calls=%async_computation.2 | async-start | bytes 524288 | tf_op jit(solution)/shard_map/all_to_all | solution.py:97
  51.8 5.2 %collective-permute-start.8 = (f32[10,34,1]{2,1,0:T(8,128)S(1)}, f32[10,34,1]{2,1,0:T(8,128)S(1)}, u32[]{:S(2)}, u32[]{:S(2)}) collective-permute-start(f32[10,34,1]{2,1,0:T(8,128)S(1)} %get-tuple-element.15), channel_id=1, source_target_pairs={{0,1},{1,2},{2,3},{4,5},{5,6},{6,7},{8,9},{9,10},{10,11},{12,13},{... | collective-permute-start | bytes 4088 | tf_op jit(solution)/shard_map/ppermute | solution.py:17
  57.0 3.8 %scatter_custom_fusion.2 = f32[256,128]{1,0:T(8,128)S(1)} fusion(s32[512]{0:T(512)S(1)} %bitcast.20, f32[512,128]{1,0:T(8,128)S(1)} %bitcast.18, f32[]{:T(128)} %constant.10.clone.1), kind=kCustom, calls=%fused_computation.209 | custom fusion | flops 65536 | bytes 131076 | tf_op jit(solution)/shard_map/scatter-add | solution.py:103
  60.8 3.8 %scatter_custom_fusion.4 = f32[256,128]{1,0:T(8,128)S(1)} fusion(s32[512]{0:T(512)S(1)} %bitcast.21, f32[512,128]{1,0:T(8,128)S(1)} %bitcast.19, f32[]{:T(128)} %constant.10.clone.1), kind=kCustom, calls=%fused_computation.207 | custom fusion | flops 65536 | bytes 131076 | tf_op jit(solution)/shard_map/scatter-add | solution.py:102
  65.1 3.7 %collective-permute-start.12 = (f32[1,32,128]{2,1,0:T(8,128)S(1)}, f32[1,32,128]{2,1,0:T(8,128)S(1)}, u32[]{:S(2)}, u32[]{:S(2)}) collective-permute-start(f32[1,32,128]{2,1,0:T(8,128)S(1)} %get-tuple-element.36), channel_id=1, source_target_pairs={{0,8},{8,16},{16,24},{1,9},{9,17},{17,25},{2,10},{10,18},{18,26},{... | collective-permute-start | bytes 49160 | tf_op jit(solution)/shard_map/ppermute | solution.py:17
  70.2 4.2 %collective-permute-done.13 = f32[1,32,128]{2,1,0:T(8,128)S(1)} collective-permute-done((f32[1,32,128]{2,1,0:T(8,128)S(1)}, f32[1,32,128]{2,1,0:T(8,128)S(1)}, u32[]{:S(2)}, u32[]{:S(2)}) %collective-permute-start.13) | collective-permute-done | bytes 16416 | tf_op jit(solution)/shard_map/ppermute | solution.py:20
  78.9 5.1 %collective-permute-start.16 = (f32[10,34,1]{2,1,0:T(8,128)S(1)}, f32[10,34,1]{2,1,0:T(8,128)S(1)}, u32[]{:S(2)}, u32[]{:S(2)}) collective-permute-start(f32[10,34,1]{2,1,0:T(8,128)S(1)} %get-tuple-element.12), channel_id=1, source_target_pairs={{0,1},{1,2},{2,3},{4,5},{5,6},{6,7},{8,9},{9,10},{10,11},{12,13},{... | collective-permute-start | bytes 4088 | tf_op jit(solution)/shard_map/ppermute | solution.py:17
  85.4 3.3 %collective-permute-done.16 = f32[10,34,1]{2,1,0:T(8,128)S(1)} collective-permute-done((f32[10,34,1]{2,1,0:T(8,128)S(1)}, f32[10,34,1]{2,1,0:T(8,128)S(1)}, u32[]{:S(2)}, u32[]{:S(2)}) %collective-permute-start.16) | collective-permute-done | bytes 1392 | tf_op jit(solution)/shard_map/ppermute | solution.py:17
  88.7 6.3 %collective-permute-done.17 = f32[10,34,1]{2,1,0:T(8,128)S(1)} collective-permute-done((f32[10,34,1]{2,1,0:T(8,128)S(1)}, f32[10,34,1]{2,1,0:T(8,128)S(1)}, u32[]{:S(2)}, u32[]{:S(2)}) %collective-permute-start.17) | collective-permute-done | bytes 1392 | tf_op jit(solution)/shard_map/ppermute | solution.py:20
  95.3 3.3 %collective-permute-start.18 = (f32[1,32,128]{2,1,0:T(8,128)S(1)}, f32[1,32,128]{2,1,0:T(8,128)S(1)}, u32[]{:S(2)}, u32[]{:S(2)}) collective-permute-start(f32[1,32,128]{2,1,0:T(8,128)S(1)} %get-tuple-element.34), channel_id=1, source_target_pairs={{0,8},{8,16},{16,24},{1,9},{9,17},{17,25},{2,10},{10,18},{18,26},{... | collective-permute-start | bytes 49160 | tf_op jit(solution)/shard_map/ppermute | solution.py:17
  100.1 4.2 %collective-permute-done.19 = f32[1,32,128]{2,1,0:T(8,128)S(1)} collective-permute-done((f32[1,32,128]{2,1,0:T(8,128)S(1)}, f32[1,32,128]{2,1,0:T(8,128)S(1)}, u32[]{:S(2)}, u32[]{:S(2)}) %collective-permute-start.19) | collective-permute-done | bytes 16416 | tf_op jit(solution)/shard_map/ppermute | solution.py:20
  108.8 2.4 %collective-permute-start.22 = (f32[10,34,1]{2,1,0:T(8,128)S(1)}, f32[10,34,1]{2,1,0:T(8,128)S(1)}, u32[]{:S(2)}, u32[]{:S(2)}) collective-permute-start(f32[10,34,1]{2,1,0:T(8,128)S(1)} %get-tuple-element.10), channel_id=1, source_target_pairs={{0,1},{1,2},{2,3},{4,5},{5,6},{6,7},{8,9},{9,10},{10,11},{12,13},{... | collective-permute-start | bytes 4088 | tf_op jit(solution)/shard_map/ppermute | solution.py:17
  112.5 3.3 %collective-permute-done.22 = f32[10,34,1]{2,1,0:T(8,128)S(1)} collective-permute-done((f32[10,34,1]{2,1,0:T(8,128)S(1)}, f32[10,34,1]{2,1,0:T(8,128)S(1)}, u32[]{:S(2)}, u32[]{:S(2)}) %collective-permute-start.22) | collective-permute-done | bytes 1392 | tf_op jit(solution)/shard_map/ppermute | solution.py:17
  115.8 5.1 %collective-permute-done.23 = f32[10,34,1]{2,1,0:T(8,128)S(1)} collective-permute-done((f32[10,34,1]{2,1,0:T(8,128)S(1)}, f32[10,34,1]{2,1,0:T(8,128)S(1)}, u32[]{:S(2)}, u32[]{:S(2)}) %collective-permute-start.23) | collective-permute-done | bytes 1392 | tf_op jit(solution)/shard_map/ppermute | solution.py:20
  121.3 3.4 %collective-permute-start.24 = (f32[1,32,128]{2,1,0:T(8,128)S(1)}, f32[1,32,128]{2,1,0:T(8,128)S(1)}, u32[]{:S(2)}, u32[]{:S(2)}) collective-permute-start(f32[1,32,128]{2,1,0:T(8,128)S(1)} %get-tuple-element.32), channel_id=1, source_target_pairs={{0,8},{8,16},{16,24},{1,9},{9,17},{17,25},{2,10},{10,18},{18,26},{... | collective-permute-start | bytes 49160 | tf_op jit(solution)/shard_map/ppermute | solution.py:17
  126.1 4.2 %collective-permute-done.25 = f32[1,32,128]{2,1,0:T(8,128)S(1)} collective-permute-done((f32[1,32,128]{2,1,0:T(8,128)S(1)}, f32[1,32,128]{2,1,0:T(8,128)S(1)}, u32[]{:S(2)}, u32[]{:S(2)}) %collective-permute-start.25) | collective-permute-done | bytes 16416 | tf_op jit(solution)/shard_map/ppermute | solution.py:20
  134.8 2.1 collective-permute-start.28
  138.2 3.3 %collective-permute-done.28 = f32[10,34,1]{2,1,0:T(8,128)S(1)} collective-permute-done((f32[10,34,1]{2,1,0:T(8,128)S(1)}, f32[10,34,1]{2,1,0:T(8,128)S(1)}, u32[]{:S(2)}, u32[]{:S(2)}) %collective-permute-start.28) | collective-permute-done | bytes 1392 | tf_op jit(solution)/shard_map/ppermute | solution.py:17
  141.5 5.1 %collective-permute-done.29 = f32[10,34,1]{2,1,0:T(8,128)S(1)} collective-permute-done((f32[10,34,1]{2,1,0:T(8,128)S(1)}, f32[10,34,1]{2,1,0:T(8,128)S(1)}, u32[]{:S(2)}, u32[]{:S(2)}) %collective-permute-start.29) | collective-permute-done | bytes 1392 | tf_op jit(solution)/shard_map/ppermute | solution.py:20
  147.0 1.9 collective-permute-start.30
  150.4 4.2 %collective-permute-done.31 = f32[1,32,128]{2,1,0:T(8,128)S(1)} collective-permute-done((f32[1,32,128]{2,1,0:T(8,128)S(1)}, f32[1,32,128]{2,1,0:T(8,128)S(1)}, u32[]{:S(2)}, u32[]{:S(2)}) %collective-permute-start.31) | collective-permute-done | bytes 16416 | tf_op jit(solution)/shard_map/ppermute | solution.py:20
  159.1 2.1 collective-permute-start.34
  162.5 3.3 %collective-permute-done.34 = f32[10,34,1]{2,1,0:T(8,128)S(1)} collective-permute-done((f32[10,34,1]{2,1,0:T(8,128)S(1)}, f32[10,34,1]{2,1,0:T(8,128)S(1)}, u32[]{:S(2)}, u32[]{:S(2)}) %collective-permute-start.34) | collective-permute-done | bytes 1392 | tf_op jit(solution)/shard_map/ppermute | solution.py:17
  165.8 5.1 %collective-permute-done.35 = f32[10,34,1]{2,1,0:T(8,128)S(1)} collective-permute-done((f32[10,34,1]{2,1,0:T(8,128)S(1)}, f32[10,34,1]{2,1,0:T(8,128)S(1)}, u32[]{:S(2)}, u32[]{:S(2)}) %collective-permute-start.35) | collective-permute-done | bytes 1392 | tf_op jit(solution)/shard_map/ppermute | solution.py:20
  171.9 37.9 %psum.7 = f32[]{:T(128)} all-reduce(f32[]{:T(128)} %fusion.5), channel_id=1, replica_groups=mesh['gx'=4,'gy'=2,'gz'=4] {'gx','gy','gz'}, use_global_device_ids=true, to_apply=%region_9.10 | all-reduce | flops 1 | bytes 8 | tf_op jit(solution)/shard_map/psum | solution.py:119
  (112 shorter events, 48.5 us)
Async XLA Ops:
  3.4 23.5 %all-to-all-start = ((s32[8,64,1]{1,2,0:T(1,128)}), s32[8,64,1]{1,2,0:T(1,128)S(1)}, u32[]{:S(2)}, u32[]{:S(2)}) async-start(s32[8,64,1]{1,2,0:T(1,128)} %bitcast), calls=%async_computation | async-start | bytes 8192 | tf_op jit(solution)/shard_map/all_to_all | solution.py:99
  10.4 22.1 %collective-permute-start.3 = (f32[1,32,128]{2,1,0:T(8,128)S(1)}, f32[1,32,128]{2,1,0:T(8,128)S(1)}, u32[]{:S(2)}, u32[]{:S(2)}) collective-permute-start(f32[1,32,128]{2,1,0:T(8,128)S(1)} %get-tuple-element.40), channel_id=1, source_target_pairs={{8,0},{16,8},{24,16},{9,1},{17,9},{25,17},{10,2},{18,10},{26,18},{... | collective-permute-start | bytes 49160 | tf_op jit(solution)/shard_map/ppermute | solution.py:20
  11.9 20.6 %collective-permute-start.1 = (f32[1,32,128]{2,1,0:T(8,128)S(1)}, f32[1,32,128]{2,1,0:T(8,128)S(1)}, u32[]{:S(2)}, u32[]{:S(2)}) collective-permute-start(f32[1,32,128]{2,1,0:T(8,128)S(1)} %get-tuple-element.41), channel_id=1, source_target_pairs={{0,8},{8,16},{16,24},{1,9},{9,17},{17,25},{2,10},{10,18},{18,26},{... | collective-permute-start | bytes 49160 | tf_op jit(solution)/shard_map/ppermute | solution.py:17
  17.5 18.8 %collective-permute-start.2 = (f32[1,32,128]{2,1,0:T(8,128)S(1)}, f32[1,32,128]{2,1,0:T(8,128)S(1)}, u32[]{:S(2)}, u32[]{:S(2)}) collective-permute-start(f32[1,32,128]{2,1,0:T(8,128)S(1)} %get-tuple-element.38), channel_id=1, source_target_pairs={{8,0},{16,8},{24,16},{9,1},{17,9},{25,17},{10,2},{18,10},{26,18},{... | collective-permute-start | bytes 49160 | tf_op jit(solution)/shard_map/ppermute | solution.py:20
  18.9 17.3 %collective-permute-start = (f32[1,32,128]{2,1,0:T(8,128)S(1)}, f32[1,32,128]{2,1,0:T(8,128)S(1)}, u32[]{:S(2)}, u32[]{:S(2)}) collective-permute-start(f32[1,32,128]{2,1,0:T(8,128)S(1)} %get-tuple-element.39), channel_id=1, source_target_pairs={{0,8},{8,16},{16,24},{1,9},{9,17},{17,25},{2,10},{10,18},{18,26},{... | collective-permute-start | bytes 49160 | tf_op jit(solution)/shard_map/ppermute | solution.py:17
  26.9 18.7 %all-to-all-start.1 = ((f32[8,64,128]{2,1,0:T(8,128)}), f32[8,64,128]{2,1,0:T(8,128)S(1)}, u32[]{:S(2)}, u32[]{:S(2)}) async-start(f32[8,64,128]{2,1,0:T(8,128)} %bitcast.2), calls=%async_computation.1 | async-start | bytes 524288 | tf_op jit(solution)/shard_map/all_to_all | solution.py:98
  32.5 8.1 %collective-permute-start.5 = (f32[10,1,128]{2,1,0:T(1,128)S(1)}, f32[10,1,128]{2,1,0:T(1,128)S(1)}, u32[]{:S(2)}, u32[]{:S(2)}) collective-permute-start(f32[10,1,128]{2,1,0:T(1,128)S(1)} %get-tuple-element.28), channel_id=1, source_target_pairs={{0,4},{1,5},{2,6},{3,7},{8,12},{9,13},{10,14},{11,15},{16,20},{17,... | collective-permute-start | bytes 15368 | tf_op jit(solution)/shard_map/ppermute | solution.py:17
  35.0 5.7 %collective-permute-start.7 = (f32[10,1,128]{2,1,0:T(1,128)S(1)}, f32[10,1,128]{2,1,0:T(1,128)S(1)}, u32[]{:S(2)}, u32[]{:S(2)}) collective-permute-start(f32[10,1,128]{2,1,0:T(1,128)S(1)} %get-tuple-element.29), channel_id=1, source_target_pairs={{4,0},{5,1},{6,2},{7,3},{12,8},{13,9},{14,10},{15,11},{20,16},{21,... | collective-permute-start | bytes 15368 | tf_op jit(solution)/shard_map/ppermute | solution.py:20
  36.3 9.2 %collective-permute-start.6 = (f32[10,1,128]{2,1,0:T(1,128)S(1)}, f32[10,1,128]{2,1,0:T(1,128)S(1)}, u32[]{:S(2)}, u32[]{:S(2)}) collective-permute-start(f32[10,1,128]{2,1,0:T(1,128)S(1)} %get-tuple-element.26), channel_id=1, source_target_pairs={{4,0},{5,1},{6,2},{7,3},{12,8},{13,9},{14,10},{15,11},{20,16},{21,... | collective-permute-start | bytes 15368 | tf_op jit(solution)/shard_map/ppermute | solution.py:20
  37.6 7.9 %collective-permute-start.4 = (f32[10,1,128]{2,1,0:T(1,128)S(1)}, f32[10,1,128]{2,1,0:T(1,128)S(1)}, u32[]{:S(2)}, u32[]{:S(2)}) collective-permute-start(f32[10,1,128]{2,1,0:T(1,128)S(1)} %get-tuple-element.27), channel_id=1, source_target_pairs={{0,4},{1,5},{2,6},{3,7},{8,12},{9,13},{10,14},{11,15},{16,20},{17,... | collective-permute-start | bytes 15368 | tf_op jit(solution)/shard_map/ppermute | solution.py:17
  40.8 23.8 %collective-permute-start.9 = (f32[10,34,1]{2,1,0:T(8,128)S(1)}, f32[10,34,1]{2,1,0:T(8,128)S(1)}, u32[]{:S(2)}, u32[]{:S(2)}) collective-permute-start(f32[10,34,1]{2,1,0:T(8,128)S(1)} %get-tuple-element.16), channel_id=1, source_target_pairs={{0,1},{1,2},{2,3},{4,5},{5,6},{6,7},{8,9},{9,10},{10,11},{12,13},{... | collective-permute-start | bytes 4088 | tf_op jit(solution)/shard_map/ppermute | solution.py:17
  44.2 20.4 %collective-permute-start.11 = (f32[10,34,1]{2,1,0:T(8,128)S(1)}, f32[10,34,1]{2,1,0:T(8,128)S(1)}, u32[]{:S(2)}, u32[]{:S(2)}) collective-permute-start(f32[10,34,1]{2,1,0:T(8,128)S(1)} %get-tuple-element.17), channel_id=1, source_target_pairs={{1,0},{2,1},{3,2},{5,4},{6,5},{7,6},{9,8},{10,9},{11,10},{13,12},{... | collective-permute-start | bytes 4088 | tf_op jit(solution)/shard_map/ppermute | solution.py:20
  45.6 15.2 %all-to-all-start.2 = ((f32[8,64,128]{2,1,0:T(8,128)}), f32[8,64,128]{2,1,0:T(8,128)S(1)}, u32[]{:S(2)}, u32[]{:S(2)}) async-start(f32[8,64,128]{2,1,0:T(8,128)} %bitcast.5), calls=%async_computation.2 | async-start | bytes 524288 | tf_op jit(solution)/shard_map/all_to_all | solution.py:97
  50.5 14.2 %collective-permute-start.10 = (f32[10,34,1]{2,1,0:T(8,128)S(1)}, f32[10,34,1]{2,1,0:T(8,128)S(1)}, u32[]{:S(2)}, u32[]{:S(2)}) collective-permute-start(f32[10,34,1]{2,1,0:T(8,128)S(1)} %get-tuple-element.14), channel_id=1, source_target_pairs={{1,0},{2,1},{3,2},{5,4},{6,5},{7,6},{9,8},{10,9},{11,10},{13,12},{... | collective-permute-start | bytes 4088 | tf_op jit(solution)/shard_map/ppermute | solution.py:20
  51.8 12.9 %collective-permute-start.8 = (f32[10,34,1]{2,1,0:T(8,128)S(1)}, f32[10,34,1]{2,1,0:T(8,128)S(1)}, u32[]{:S(2)}, u32[]{:S(2)}) collective-permute-start(f32[10,34,1]{2,1,0:T(8,128)S(1)} %get-tuple-element.15), channel_id=1, source_target_pairs={{0,1},{1,2},{2,3},{4,5},{5,6},{6,7},{8,9},{9,10},{10,11},{12,13},{... | collective-permute-start | bytes 4088 | tf_op jit(solution)/shard_map/ppermute | solution.py:17
  65.1 5.1 %collective-permute-start.12 = (f32[1,32,128]{2,1,0:T(8,128)S(1)}, f32[1,32,128]{2,1,0:T(8,128)S(1)}, u32[]{:S(2)}, u32[]{:S(2)}) collective-permute-start(f32[1,32,128]{2,1,0:T(8,128)S(1)} %get-tuple-element.36), channel_id=1, source_target_pairs={{0,8},{8,16},{16,24},{1,9},{9,17},{17,25},{2,10},{10,18},{18,26},{... | collective-permute-start | bytes 49160 | tf_op jit(solution)/shard_map/ppermute | solution.py:17
  68.8 5.6 %collective-permute-start.13 = (f32[1,32,128]{2,1,0:T(8,128)S(1)}, f32[1,32,128]{2,1,0:T(8,128)S(1)}, u32[]{:S(2)}, u32[]{:S(2)}) collective-permute-start(f32[1,32,128]{2,1,0:T(8,128)S(1)} %get-tuple-element.37), channel_id=1, source_target_pairs={{8,0},{16,8},{24,16},{9,1},{17,9},{25,17},{10,2},{18,10},{26,18},{... | collective-permute-start | bytes 49160 | tf_op jit(solution)/shard_map/ppermute | solution.py:20
  75.7 3.1 %collective-permute-start.15 = (f32[10,1,128]{2,1,0:T(1,128)S(1)}, f32[10,1,128]{2,1,0:T(1,128)S(1)}, u32[]{:S(2)}, u32[]{:S(2)}) collective-permute-start(f32[10,1,128]{2,1,0:T(1,128)S(1)} %get-tuple-element.25), channel_id=1, source_target_pairs={{4,0},{5,1},{6,2},{7,3},{12,8},{13,9},{14,10},{15,11},{20,16},{21,... | collective-permute-start | bytes 15368 | tf_op jit(solution)/shard_map/ppermute | solution.py:20
  78.9 9.8 %collective-permute-start.16 = (f32[10,34,1]{2,1,0:T(8,128)S(1)}, f32[10,34,1]{2,1,0:T(8,128)S(1)}, u32[]{:S(2)}, u32[]{:S(2)}) collective-permute-start(f32[10,34,1]{2,1,0:T(8,128)S(1)} %get-tuple-element.12), channel_id=1, source_target_pairs={{0,1},{1,2},{2,3},{4,5},{5,6},{6,7},{8,9},{9,10},{10,11},{12,13},{... | collective-permute-start | bytes 4088 | tf_op jit(solution)/shard_map/ppermute | solution.py:17
  84.1 10.9 %collective-permute-start.17 = (f32[10,34,1]{2,1,0:T(8,128)S(1)}, f32[10,34,1]{2,1,0:T(8,128)S(1)}, u32[]{:S(2)}, u32[]{:S(2)}) collective-permute-start(f32[10,34,1]{2,1,0:T(8,128)S(1)} %get-tuple-element.13), channel_id=1, source_target_pairs={{1,0},{2,1},{3,2},{5,4},{6,5},{7,6},{9,8},{10,9},{11,10},{13,12},{... | collective-permute-start | bytes 4088 | tf_op jit(solution)/shard_map/ppermute | solution.py:20
  95.3 4.7 %collective-permute-start.18 = (f32[1,32,128]{2,1,0:T(8,128)S(1)}, f32[1,32,128]{2,1,0:T(8,128)S(1)}, u32[]{:S(2)}, u32[]{:S(2)}) collective-permute-start(f32[1,32,128]{2,1,0:T(8,128)S(1)} %get-tuple-element.34), channel_id=1, source_target_pairs={{0,8},{8,16},{16,24},{1,9},{9,17},{17,25},{2,10},{10,18},{18,26},{... | collective-permute-start | bytes 49160 | tf_op jit(solution)/shard_map/ppermute | solution.py:17
  98.6 5.6 %collective-permute-start.19 = (f32[1,32,128]{2,1,0:T(8,128)S(1)}, f32[1,32,128]{2,1,0:T(8,128)S(1)}, u32[]{:S(2)}, u32[]{:S(2)}) collective-permute-start(f32[1,32,128]{2,1,0:T(8,128)S(1)} %get-tuple-element.35), channel_id=1, source_target_pairs={{8,0},{16,8},{24,16},{9,1},{17,9},{25,17},{10,2},{18,10},{26,18},{... | collective-permute-start | bytes 49160 | tf_op jit(solution)/shard_map/ppermute | solution.py:20
  108.8 7.0 %collective-permute-start.22 = (f32[10,34,1]{2,1,0:T(8,128)S(1)}, f32[10,34,1]{2,1,0:T(8,128)S(1)}, u32[]{:S(2)}, u32[]{:S(2)}) collective-permute-start(f32[10,34,1]{2,1,0:T(8,128)S(1)} %get-tuple-element.10), channel_id=1, source_target_pairs={{0,1},{1,2},{2,3},{4,5},{5,6},{6,7},{8,9},{9,10},{10,11},{12,13},{... | collective-permute-start | bytes 4088 | tf_op jit(solution)/shard_map/ppermute | solution.py:17
  111.2 9.8 %collective-permute-start.23 = (f32[10,34,1]{2,1,0:T(8,128)S(1)}, f32[10,34,1]{2,1,0:T(8,128)S(1)}, u32[]{:S(2)}, u32[]{:S(2)}) collective-permute-start(f32[10,34,1]{2,1,0:T(8,128)S(1)} %get-tuple-element.11), channel_id=1, source_target_pairs={{1,0},{2,1},{3,2},{5,4},{6,5},{7,6},{9,8},{10,9},{11,10},{13,12},{... | collective-permute-start | bytes 4088 | tf_op jit(solution)/shard_map/ppermute | solution.py:20
  121.3 4.8 %collective-permute-start.24 = (f32[1,32,128]{2,1,0:T(8,128)S(1)}, f32[1,32,128]{2,1,0:T(8,128)S(1)}, u32[]{:S(2)}, u32[]{:S(2)}) collective-permute-start(f32[1,32,128]{2,1,0:T(8,128)S(1)} %get-tuple-element.32), channel_id=1, source_target_pairs={{0,8},{8,16},{16,24},{1,9},{9,17},{17,25},{2,10},{10,18},{18,26},{... | collective-permute-start | bytes 49160 | tf_op jit(solution)/shard_map/ppermute | solution.py:17
  124.7 5.6 %collective-permute-start.25 = (f32[1,32,128]{2,1,0:T(8,128)S(1)}, f32[1,32,128]{2,1,0:T(8,128)S(1)}, u32[]{:S(2)}, u32[]{:S(2)}) collective-permute-start(f32[1,32,128]{2,1,0:T(8,128)S(1)} %get-tuple-element.33), channel_id=1, source_target_pairs={{8,0},{16,8},{24,16},{9,1},{17,9},{25,17},{10,2},{18,10},{26,18},{... | collective-permute-start | bytes 49160 | tf_op jit(solution)/shard_map/ppermute | solution.py:20
  134.8 6.7 %collective-permute-start.28 = (f32[10,34,1]{2,1,0:T(8,128)S(1)}, f32[10,34,1]{2,1,0:T(8,128)S(1)}, u32[]{:S(2)}, u32[]{:S(2)}) collective-permute-start(f32[10,34,1]{2,1,0:T(8,128)S(1)} %get-tuple-element.8), channel_id=1, source_target_pairs={{0,1},{1,2},{2,3},{4,5},{5,6},{6,7},{8,9},{9,10},{10,11},{12,13},{... | collective-permute-start | bytes 4088 | tf_op jit(solution)/shard_map/ppermute | solution.py:17
  136.9 9.8 %collective-permute-start.29 = (f32[10,34,1]{2,1,0:T(8,128)S(1)}, f32[10,34,1]{2,1,0:T(8,128)S(1)}, u32[]{:S(2)}, u32[]{:S(2)}) collective-permute-start(f32[10,34,1]{2,1,0:T(8,128)S(1)} %get-tuple-element.9), channel_id=1, source_target_pairs={{1,0},{2,1},{3,2},{5,4},{6,5},{7,6},{9,8},{10,9},{11,10},{13,12},{... | collective-permute-start | bytes 4088 | tf_op jit(solution)/shard_map/ppermute | solution.py:20
  147.0 3.4 %collective-permute-start.30 = (f32[1,32,128]{2,1,0:T(8,128)S(1)}, f32[1,32,128]{2,1,0:T(8,128)S(1)}, u32[]{:S(2)}, u32[]{:S(2)}) collective-permute-start(f32[1,32,128]{2,1,0:T(8,128)S(1)} %get-tuple-element.30), channel_id=1, source_target_pairs={{0,8},{8,16},{16,24},{1,9},{9,17},{17,25},{2,10},{10,18},{18,26},{... | collective-permute-start | bytes 49160 | tf_op jit(solution)/shard_map/ppermute | solution.py:17
  148.9 5.6 %collective-permute-start.31 = (f32[1,32,128]{2,1,0:T(8,128)S(1)}, f32[1,32,128]{2,1,0:T(8,128)S(1)}, u32[]{:S(2)}, u32[]{:S(2)}) collective-permute-start(f32[1,32,128]{2,1,0:T(8,128)S(1)} %get-tuple-element.31), channel_id=1, source_target_pairs={{8,0},{16,8},{24,16},{9,1},{17,9},{25,17},{10,2},{18,10},{26,18},{... | collective-permute-start | bytes 49160 | tf_op jit(solution)/shard_map/ppermute | solution.py:20
  159.1 6.7 %collective-permute-start.34 = (f32[10,34,1]{2,1,0:T(8,128)S(1)}, f32[10,34,1]{2,1,0:T(8,128)S(1)}, u32[]{:S(2)}, u32[]{:S(2)}) collective-permute-start(f32[10,34,1]{2,1,0:T(8,128)S(1)} %get-tuple-element.6), channel_id=1, source_target_pairs={{0,1},{1,2},{2,3},{4,5},{5,6},{6,7},{8,9},{9,10},{10,11},{12,13},{... | collective-permute-start | bytes 4088 | tf_op jit(solution)/shard_map/ppermute | solution.py:17
  161.2 9.8 %collective-permute-start.35 = (f32[10,34,1]{2,1,0:T(8,128)S(1)}, f32[10,34,1]{2,1,0:T(8,128)S(1)}, u32[]{:S(2)}, u32[]{:S(2)}) collective-permute-start(f32[10,34,1]{2,1,0:T(8,128)S(1)} %get-tuple-element.7), channel_id=1, source_target_pairs={{1,0},{2,1},{3,2},{5,4},{6,5},{7,6},{9,8},{10,9},{11,10},{13,12},{... | collective-permute-start | bytes 4088 | tf_op jit(solution)/shard_map/ppermute | solution.py:20
  (16 other events, 89.0 us)
where the time goes:
time: 213 us; the launch traced here: 212 us
  starting transfers between devices  91.1 us (43%)
  waiting for transfers between devices  59.4 us (28%)
  blocking collectives  37.9 us (18%)
  other arithmetic  14.5 us (7%)
  local copies, waits for them, and re-layouts  5.41 us (3%)
  between operations  3.21 us (2%)
    ppermute x18, starting transfers between devices, with_halo(): lax.ppermute(lax.slice_in_dim(block, block.shape[dim] - width, None, axis...  52.2 us
    ppermute x18, waiting for transfers between devices, with_halo(): lax.ppermute(lax.slice_in_dim(block, 0, width, axis=dim), axis, backward)  45.5 us
    psum x1, blocking collectives, on_device(): squared_total = lax.psum(jnp.sum(residual * residual), ('gx', 'gy', 'gz'))  37.9 us
    ppermute x18, starting transfers between devices, with_halo(): lax.ppermute(lax.slice_in_dim(block, 0, width, axis=dim), axis, backward)  23.5 us
    ppermute x18, waiting for transfers between devices, with_halo(): lax.ppermute(lax.slice_in_dim(block, block.shape[dim] - width, None, axis...  13.9 us
    all_to_all x1, starting transfers between devices, on_device(): lax.all_to_all(column_buf, ('gx', 'gy'), split_axis=0, concat_axis=0, til...  6.33 us
    all_to_all x1, starting transfers between devices, on_device(): lax.all_to_all(cond_buf, ('gx', 'gy'), split_axis=0, concat_axis=0, tiled...  4.75 us
    all_to_all x1, starting transfers between devices, on_device(): lax.all_to_all(extra_buf, ('gx', 'gy'), split_axis=0, concat_axis=0, tile...  4.32 us
  transfers between devices with their start and end apart: 39, of which 20 were waited for; matrix products, arithmetic and copies ran while one was open for 7% of the time, Pallas kernels for 0%

commit v1 on v0

v1 whole, which is shorter than its diff:
```python
import functools

import jax
import jax.numpy as jnp
from jax import lax
from jax.experimental import pallas as pl
from jax.experimental.pallas import tpu as pltpu
from jax.sharding import PartitionSpec as P

SWEEPS = 4
RELAX = 0.8
MESH = pl.DeviceIdType.MESH
F32 = jnp.float32
BF16 = jnp.bfloat16


def each(low, high, body):
    if high - low <= 16:
        for k in range(low, high):
            body(k)
    else:
        def step(k, carry):
            body(k)
            return carry
        lax.fori_loop(low, high, step, 0)


def terms(value):
    high = value.astype(BF16).astype(F32)
    rest = value - high
    mid = rest.astype(BF16).astype(F32)
    return high, mid, rest - mid


def kernel(
    sizes,
    eps_ref,
    charge_ref,
    texture_ref,
    layer_ref,
    volts_ref,
    cond_ref,
    gate_ref,
    dest_ref,
    column_ref,
    initial_ref,
    out_ref,
    norm_ref,
    field,
    coef,
    blocks_out,
    blocks_in,
    face_y,
    face_z,
    halo_x,
    halo_y,
    halo_z,
    coupled,
    part,
    sums,
    part2,
    sums2,
    block_send,
    block_recv,
    face_send,
    face_recv,
    sum_send,
    sum_recv,
    sum2_send,
    sum2_recv,
):
    grid_x, grid_y, grid_z, capacity, used = sizes
    peers = grid_x * grid_y
    cx, cy, cz = charge_ref.shape
    exchanges = SWEEPS + 2
    ix, iy, iz = lax.axis_index("gx"), lax.axis_index("gy"), lax.axis_index("gz")
    me = ix * grid_y + iy
    here = (ix, iy, iz)
    counts = (grid_x, grid_y, grid_z)
    names = ("gx", "gy", "gz")

    def peer(k):
        target = lax.rem(me + k, peers)
        return target, {"gx": target // grid_y, "gy": lax.rem(target, grid_y)}

    def layer(k):
        return {"gz": lax.rem(iz + k, grid_z)}

    def beside(axis, side):
        return here[axis] > 0 if side == 0 else here[axis] < counts[axis] - 1

    for axis, halo in enumerate((halo_x, halo_y, halo_z)):
        for side in range(2):
            @pl.when(jnp.logical_not(beside(axis, side)))
            def _(halo=halo, side=side):
                halo[:, side] = jnp.zeros(halo.shape[:1] + halo.shape[2:], F32)

    barrier = pltpu.get_barrier_semaphore()
    each(1, peers, lambda k: pl.semaphore_signal(barrier, inc=1, device_id=peer(k)[1], device_id_type=MESH))
    each(1, grid_z, lambda k: pl.semaphore_signal(barrier, inc=1, device_id=layer(k), device_id_type=MESH))

    lane = lax.broadcasted_iota(jnp.int32, (cy, cz), 1)

    def pack(exchange, value):
        face_y[exchange, 0] = value[:, 0, :]
        face_y[exchange, 1] = value[:, cy - 1, :]
        faces = jnp.zeros((cy, cz), F32)
        for x in range(cx):
            faces = jnp.where(lane == x, value[x, :, cz - 1:cz], faces)
            faces = jnp.where(lane == cx + x, value[x, :, 0:1], faces)
        face_z[exchange] = faces

    def face_copy(exchange, axis, side):
        step = counts[axis] - 1 if side == 0 else 1
        if axis == 0:
            source, target = field.at[exchange, 0 if side == 0 else cx - 1], halo_x
        elif axis == 1:
            source, target = face_y.at[exchange, side], halo_y
        else:
            source, target = face_z.at[exchange], halo_z
        return pltpu.make_async_remote_copy(
            src_ref=source,
            dst_ref=target.at[exchange, 1 - side],
            send_sem=face_send.at[exchange, 2 * axis + side],
            recv_sem=face_recv.at[exchange, 2 * axis + 1 - side],
            device_id={names[axis]: lax.rem(here[axis] + step, counts[axis])},
            device_id_type=MESH,
        )

    def send_faces(exchange):
        for axis in (2, 0, 1):
            for side in range(2):
                @pl.when(beside(axis, side))
                def _(axis=axis, side=side):
                    face_copy(exchange, axis, side).start()

    def wait_faces(exchange):
        for axis in (1, 0, 2):
            for side in range(2):
                @pl.when(beside(axis, side))
                def _(axis=axis, side=side):
                    face_copy(exchange, axis, 1 - side).wait_recv()

    row_y = lax.broadcasted_iota(jnp.int32, (cx, cy, cz), 1)
    lane3 = lax.broadcasted_iota(jnp.int32, (cx, cy, cz), 2)

    def shifted(exchange, value):
        low_x = jnp.concatenate([halo_x[exchange, 0][None], value[:-1]], axis=0)
        high_x = jnp.concatenate([value[1:], halo_x[exchange, 1][None]], axis=0)
        low_y = jnp.where(row_y == 0, halo_y[exchange, 0][:, None, :], pltpu.roll(value, 1, 1))
        high_y = jnp.where(row_y == cy - 1, halo_y[exchange, 1][:, None, :], pltpu.roll(value, cy - 1, 1))
        low_face, high_face = halo_z[exchange, 0], halo_z[exchange, 1]
        low_z = jnp.stack([jnp.broadcast_to(low_face[:, x:x + 1], (cy, cz)) for x in range(cx)])
        high_z = jnp.stack([jnp.broadcast_to(high_face[:, cx + x:cx + x + 1], (cy, cz)) for x in range(cx)])
        low_z = jnp.where(lane3 == 0, low_z, pltpu.roll(value, 1, 2))
        high_z = jnp.where(lane3 == cz - 1, high_z, pltpu.roll(value, cz - 1, 2))
        return low_x, high_x, low_y, high_y, low_z, high_z

    layers = layer_ref[...]
    layer_eps = jnp.zeros(layers.shape, F32)
    for m in range(eps_ref.shape[0]):
        layer_eps = jnp.where(layers == m, eps_ref[m], layer_eps)
    permittivity = texture_ref[...] * layer_eps[None]
    field[0] = permittivity
    pack(0, permittivity)
    initial = initial_ref[...]
    field[1] = initial
    pack(1, initial)

    count = cond_ref.shape[0]
    down = lax.broadcasted_iota(jnp.int32, (count, count), 0)
    across = lax.broadcasted_iota(jnp.int32, (count, count), 1)

    def upright(row):
        return jnp.sum(jnp.where(down == across, row, jnp.zeros_like(row)), axis=1, keepdims=True)

    dest_row = dest_ref[...].astype(F32)
    dest_col = upright(dest_row)
    same = dest_row == dest_col
    rank_row = jnp.sum(jnp.where(same & (down < across), 1.0, 0.0), axis=0, keepdims=True)
    position_row = dest_row * capacity + rank_row
    position_col = upright(position_row)
    gate_col = upright(gate_ref[...].astype(F32)).astype(jnp.int32)
    gates = volts_ref.shape[1]
    gate_ids = lax.broadcasted_iota(jnp.int32, (count, gates), 1)
    volts_col = jnp.sum(jnp.where(gate_ids == gate_col, volts_ref[...], 0.0), axis=1, keepdims=True)
    column_col = upright(column_ref[...].astype(F32))

    slots = peers * capacity
    slot = lax.broadcasted_iota(jnp.int32, (slots, count), 0)
    chosen = jnp.where(slot == position_row.astype(jnp.int32), 1.0, 0.0).astype(BF16)
    high, mid, low = terms(cond_ref[...])
    pair = jnp.concatenate([high, mid], axis=1).astype(BF16)
    moved = jnp.dot(chosen, pair, preferred_element_type=F32)
    moved_low = jnp.dot(chosen, low.astype(BF16), preferred_element_type=F32)
    moved = moved[:, :cz] + moved[:, cz:] + moved_low
    blocks_out[:, :capacity, :] = moved.reshape(peers, capacity, cz)
    place = lax.rem(across, capacity)
    position_int = position_col.astype(jnp.int32)

    def details(p):
        mine = position_int == place + p * capacity
        blocks_out[p, capacity:capacity + 1, :] = jnp.sum(jnp.where(mine, column_col, 0.0), axis=0, keepdims=True)
        blocks_out[p, capacity + 1:capacity + 2, :] = jnp.sum(jnp.where(mine, volts_col, 0.0), axis=0, keepdims=True)

    blocks_out[:, capacity + 2:, :] = jnp.zeros((peers, 6, cz), F32)
    each(0, peers, details)

    pl.semaphore_wait(barrier, peers - 1 + grid_z - 1)

    def block_copy(k):
        target, device = peer(k)
        return pltpu.make_async_remote_copy(
            src_ref=blocks_out.at[target],
            dst_ref=blocks_in.at[k],
            send_sem=block_send.at[k],
            recv_sem=block_recv.at[k],
            device_id=device,
            device_id_type=MESH,
        )

    send_faces(0)
    send_faces(1)
    each(1, peers, lambda k: block_copy(k).start())

    columns = cx * cy
    depth = -(-3 * capacity // cz) * cz
    column_ids = lax.broadcasted_iota(jnp.int32, (columns, cz), 0)
    eye = lax.broadcasted_iota(jnp.int32, (capacity, cz), 0) == lax.broadcasted_iota(jnp.int32, (capacity, cz), 1)

    def product(blocks):
        cond = blocks[:capacity]
        row = blocks[capacity:capacity + 1].astype(jnp.int32)
        volts = jnp.sum(jnp.where(eye, blocks[capacity + 1:capacity + 2], 0.0), axis=1, keepdims=True)
        both = jnp.concatenate([cond, cond * volts], axis=1)
        pieces = list(terms(both))
        if depth > 3 * capacity:
            pieces.append(jnp.zeros((depth - 3 * capacity, 2 * cz), F32))
        right = jnp.concatenate(pieces, axis=0).astype(BF16)
        hit = jnp.where(column_ids == row, 1.0, 0.0).astype(BF16)
        left = jnp.concatenate([hit] * (depth // cz), axis=1)
        return jnp.dot(left, right, preferred_element_type=F32)

    coupled[...] = product(blocks_out[me])

    wait_faces(0)
    coefficients = []
    for neighbour in shifted(0, permittivity):
        coefficients.append(2.0 * permittivity * neighbour / (permittivity + neighbour))
    diagonal = coefficients[0]
    for index in range(1, 6):
        diagonal = diagonal + coefficients[index]
    for index in range(6):
        coef[index] = coefficients[index]
    wait_faces(1)

    def neighbours(exchange, value):
        pieces = shifted(exchange, value)
        total = coef[0] * pieces[0]
        for index in range(1, 6):
            total = total + coef[index] * pieces[index]
        return total

    first = neighbours(1, initial_ref[...]) + charge_ref[...]
    coef[6] = first
    coef[7] = diagonal

    def arrive(k):
        block_copy(k).wait_recv()
        coupled[...] += product(blocks_in[k])

    each(1, peers, arrive)
    diagonal = coef[7] + coupled[:, :cz].reshape(cx, cy, cz)
    injected = coupled[:, cz:].reshape(cx, cy, cz)
    scale = RELAX / diagonal
    potential = (1.0 - RELAX) * initial_ref[...] + scale * (coef[6] + injected)
    field[2] = potential
    pack(2, potential)
    send_faces(2)
    for index in range(6):
        coef[index] = coef[index] * scale
    forcing = (charge_ref[...] + injected) * scale
    coef[6] = forcing
    coef[7] = diagonal * (1.0 / RELAX)

    for exchange in range(2, exchanges - 1):
        wait_faces(exchange)
        potential = field[exchange]
        potential = (1.0 - RELAX) * potential + (coef[6] + neighbours(exchange, potential))
        field[exchange + 1] = potential
        pack(exchange + 1, potential)
        send_faces(exchange + 1)

    last = exchanges - 1
    out_ref[...] = field[last]
    wait_faces(last)
    potential = field[last]
    residual = (coef[6] + neighbours(last, potential) - RELAX * potential) * coef[7]
    squares = jnp.sum(residual * residual, axis=0)
    total = squares[:8]
    for y in range(8, cy, 8):
        total = total + squares[y:y + 8]

    part[...] = total
    sums[me] = total

    def sum_copy(k):
        return pltpu.make_async_remote_copy(
            src_ref=part,
            dst_ref=sums.at[me],
            send_sem=sum_send.at[k],
            recv_sem=sum_recv.at[k],
            device_id=peer(k)[1],
            device_id_type=MESH,
        )

    def sum2_copy(k):
        return pltpu.make_async_remote_copy(
            src_ref=part2,
            dst_ref=sums2.at[iz],
            send_sem=sum2_send.at[k],
            recv_sem=sum2_recv.at[k],
            device_id=layer(k),
            device_id_type=MESH,
        )

    each(1, peers, lambda k: sum_copy(k).start())
    each(1, peers, lambda k: sum_copy(k).wait_recv())
    total = jnp.sum(sums[...], axis=0)
    part2[...] = total
    sums2[iz] = total
    each(1, grid_z, lambda k: sum2_copy(k).start())
    each(1, peers, lambda k: block_copy(k).wait_send())
    for exchange in range(exchanges):
        for axis in range(3):
            for side in range(2):
                @pl.when(beside(axis, side))
                def _(exchange=exchange, axis=axis, side=side):
                    face_copy(exchange, axis, side).wait_send()
    each(1, peers, lambda k: sum_copy(k).wait_send())
    each(1, grid_z, lambda k: sum2_copy(k).wait_recv())
    total = jnp.sum(sums2[...], axis=0)
    cells = cx * cy * cz * grid_x * grid_y * grid_z
    norm_ref[...] = jnp.sqrt(jnp.sum(total, keepdims=True) / cells)
    each(1, grid_z, lambda k: sum2_copy(k).wait_send())


def on_device(
    sizes,
    charge,
    texture,
    material_eps,
    layer_material,
    gate_volts,
    block_cond,
    block_gate,
    block_dest,
    block_column,
    initial,
):
    grid_x, grid_y, grid_z, capacity, _ = sizes
    peers = grid_x * grid_y
    cx, cy, cz = charge.shape
    exchanges = SWEEPS + 2
    vmem = pl.BlockSpec(memory_space=pltpu.VMEM)
    dma = pltpu.SemaphoreType.DMA
    potential, norm = pl.pallas_call(
        functools.partial(kernel, sizes),
        out_shape=(jax.ShapeDtypeStruct(charge.shape, F32), jax.ShapeDtypeStruct((1, 1), F32)),
        in_specs=[pl.BlockSpec(memory_space=pltpu.SMEM)] + [vmem] * 9,
        out_specs=(vmem, vmem),
        scratch_shapes=[
            pltpu.VMEM((exchanges, cx, cy, cz), F32),
            pltpu.VMEM((8, cx, cy, cz), F32),
            pltpu.VMEM((peers, capacity + 8, cz), F32),
            pltpu.VMEM((peers, capacity + 8, cz), F32),
            pltpu.VMEM((exchanges, 2, cx, cz), F32),
            pltpu.VMEM((exchanges, cy, cz), F32),
            pltpu.VMEM((exchanges, 2, cy, cz), F32),
            pltpu.VMEM((exchanges, 2, cx, cz), F32),
            pltpu.VMEM((exchanges, 2, cy, cz), F32),
            pltpu.VMEM((cx * cy, 2 * cz), F32),
            pltpu.VMEM((8, cz), F32),
            pltpu.VMEM((peers, 8, cz), F32),
            pltpu.VMEM((8, cz), F32),
            pltpu.VMEM((grid_z, 8, cz), F32),
            dma((peers,)),
            dma((peers,)),
            dma((exchanges, 6)),
            dma((exchanges, 6)),
            dma((peers,)),
            dma((peers,)),
            dma((grid_z,)),
            dma((grid_z,)),
        ],
        compiler_params=pltpu.CompilerParams(
            collective_id=0, has_side_effects=True, vmem_limit_bytes=32 * 1024 * 1024
        ),
    )(
        material_eps,
        charge,
        texture,
        layer_material[None, :],
        gate_volts[None, :],
        block_cond,
        block_gate[None, :],
        block_dest[None, :],
        block_column[None, :],
        initial,
    )
    return potential, norm[0, 0]


def solution(mesh):
    grid_x, grid_y, grid_z = mesh.shape["gx"], mesh.shape["gy"], mesh.shape["gz"]
    peers = grid_x * grid_y

    def program(*arrays):
        count = arrays[5].shape[0] // (peers * grid_z)
        used = max(2, 4 * count // peers)
        capacity = -(-used // 8) * 8
        sizes = (grid_x, grid_y, grid_z, capacity, used)
        in_specs = (
            P("gx", "gy", "gz"),
            P("gx", "gy", "gz"),
            P(),
            P("gz"),
            P(),
            P(("gx", "gy", "gz"), None),
            P(("gx", "gy", "gz")),
            P(("gx", "gy", "gz")),
            P(("gx", "gy", "gz")),
            P("gx", "gy", "gz"),
        )
        return jax.shard_map(
            functools.partial(on_device, sizes),
            mesh=mesh,
            in_specs=in_specs,
            out_specs=(P("gx", "gy", "gz"), P()),
            check_vma=False,
        )(*arrays)

    return program
```

time: 213 us -> 45.7 us (0.21)
  starting transfers between devices: 91.1 us -> 0 us
  waiting for transfers between devices: 59.4 us -> 0 us
  Pallas kernels: 0 us -> 38.1 us
  blocking collectives: 37.9 us -> 0 us
  other arithmetic: 14.5 us -> 0 us
    ppermute x36 -> x0, starting transfers between devices: 75.7 us -> none  [the longest x18 52.2 us: with_halo(): lax.ppermute(lax.slice_in_dim(block, block.shape[dim] - width, None, axis...]
    ppermute x36 -> x0, waiting for transfers between devices: 59.4 us -> none  [the longest x18 45.5 us: with_halo(): lax.ppermute(lax.slice_in_dim(block, 0, width, axis=dim), axis, backward)]
    pallas_call x0 -> x1, Pallas kernels: none -> 38.1 us  [on_device(): pl.pallas_call(functools.partial(kernel, sizes), out_shape=(jax.ShapeDtyp...]
    psum x1 -> x0, blocking collectives: 37.9 us -> none  [on_device(): squared_total = lax.psum(jnp.sum(residual * residual), ('gx', 'gy', 'gz'))]
    all_to_all x3 -> x0, starting transfers between devices: 15.4 us -> none  [the longest x1 6.33 us: on_device(): lax.all_to_all(column_buf, ('gx', 'gy'), split_axis=0, concat_axis=0, til...]
    scatter-add x2 -> x0, other arithmetic: 7.61 us -> none  [the longest x1 3.8 us: on_device(): empty.at[column_recv].add(extra_recv).reshape(cells_x, cells_y, cells_z)]
    unnamed x20 -> x21, local copies, waits for them, and re-layouts: 0.06 us -> 4.89 us
    scatter x2 -> x0, local copies, waits for them, and re-layouts: 2.66 us -> none  [the longest x1 1.55 us: on_device(): jnp.zeros((slot_total, cells_z), jnp.float32).at[position].set(block_cond)]
  transfers between devices with their start and end apart: 39 -> 0, of which waited for: 20 -> 0; matrix products, arithmetic and copies ran while one was open for 7% -> 0% of each run, Pallas kernels for 0% -> 0%
where the time goes in v1:
time: 45.7 us; the launch traced here: 45.5 us
  Pallas kernels  38.1 us (83%)
  local copies, waits for them, and re-layouts  4.89 us (11%)
  between operations  2.46 us (5%)
    pallas_call x1, Pallas kernels, on_device(): pl.pallas_call(functools.partial(kernel, sizes), out_shape=(jax.ShapeDtyp...  38.1 us
    unnamed x21, local copies, waits for them, and re-layouts  4.89 us

profile of v1, /device:TPU:0, one launch (start us, length us, event | category | flops | bytes accessed | tf_op | source)
XLA Modules:
  0.0 45.5 jit_solution(11278513788046831811)
XLA Ops:
  0.6 0.0 copy-start.4
  0.6 0.0 copy-start.8
  0.7 0.0 copy-start.9
  0.7 0.0 copy-start.5
  0.7 0.0 copy-start.6
  0.7 0.0 copy-start.7
  0.7 0.6 %copy-done.4 = f32[1000]{0:T(1024)S(1)} copy-done((f32[1000]{0:T(1024)S(1)}, f32[1000]{0:T(1024)}, u32[]{:S(2)}) %copy-start.4) | copy-done | bytes 4024
  1.3 0.0 copy-done.8
  1.3 0.0 copy-done.9
  1.3 0.0 copy-done.5
  1.3 0.0 copy-done.6
  1.4 0.0 copy-done.7
  1.4 0.0 copy-start
  1.4 0.9 %copy-done = f32[8,32,128]{2,1,0:T(8,128)S(1)} copy-done((f32[8,32,128]{2,1,0:T(8,128)S(1)}, f32[8,32,128]{2,1,0:T(8,128)}, u32[]{:S(2)}) %copy-start) | copy-done | bytes 131096
  2.3 0.0 copy-start.1
  2.3 0.9 %copy-done.1 = f32[8,32,128]{2,1,0:T(8,128)S(1)} copy-done((f32[8,32,128]{2,1,0:T(8,128)S(1)}, f32[8,32,128]{2,1,0:T(8,128)}, u32[]{:S(2)}) %copy-start.1) | copy-done | bytes 131096
  3.2 0.0 copy-start.2
  3.2 0.9 %copy-done.2 = f32[8,32,128]{2,1,0:T(8,128)S(1)} copy-done((f32[8,32,128]{2,1,0:T(8,128)S(1)}, f32[8,32,128]{2,1,0:T(8,128)}, u32[]{:S(2)}) %copy-start.2) | copy-done | bytes 131096
  4.1 0.0 copy-start.3
  4.1 0.8 %copy-done.3 = f32[128,128]{1,0:T(8,128)S(1)} copy-done((f32[128,128]{1,0:T(8,128)S(1)}, f32[128,128]{1,0:T(8,128)}, u32[]{:S(2)}) %copy-start.3) | copy-done | bytes 65560
  4.9 38.1 %shard_map.113 = (f32[8,32,128]{2,1,0:T(8,128)S(1)}, f32[1,1]{1,0:T(1,128)}) custom-call(f32[6]{0:T(128)S(1)} %copy-done.5, f32[8,32,128]{2,1,0:T(8,128)S(1)} %copy-done, f32[8,32,128]{2,1,0:T(8,128)S(1)} %copy-done.1, s32[1,128]{1,0:T(1,128)S(1)} %bitcast.7, f32[1,1000]{1,0:T(1,128)S(1)} %bitcast.6, f32[128,128]{1,0:T(8,128)S(1)} %copy-done.3, ...), custom_call_target="tpu_custom_call" | custom-call | tf_op jit(solution)/shard_map/pallas_call | solution.py:367
  43.1 0.7 %copy.14 = f32[8,32,128]{2,1,0:T(8,128)} copy(f32[8,32,128]{2,1,0:T(8,128)S(1)} %get-tuple-element.8) | data formatting | bytes 262144
Async XLA Ops:
  0.6 0.7 %copy-start.4 = (f32[1000]{0:T(1024)S(1)}, f32[1000]{0:T(1024)}, u32[]{:S(2)}) copy-start(f32[1000]{0:T(1024)} %param.14) | copy-start | bytes 12004
  0.6 0.7 %copy-start.8 = (s32[128]{0:T(128)S(1)}, s32[128]{0:T(128)}, u32[]{:S(2)}) copy-start(s32[128]{0:T(128)} %param.17) | copy-start | bytes 1540
  0.7 0.7 %copy-start.9 = (s32[128]{0:T(128)S(1)}, s32[128]{0:T(128)}, u32[]{:S(2)}) copy-start(s32[128]{0:T(128)} %param.18) | copy-start | bytes 1540
  0.7 0.7 %copy-start.5 = (f32[6]{0:T(128)S(1)}, f32[6]{0:T(128)}, u32[]{:S(2)}) copy-start(f32[6]{0:T(128)} %eps_ref.1) | copy-start | bytes 76
  0.7 0.7 %copy-start.6 = (s32[128]{0:T(128)S(1)}, s32[128]{0:T(128)}, u32[]{:S(2)}) copy-start(s32[128]{0:T(128)} %param.13) | copy-start | bytes 1540
  0.7 0.7 %copy-start.7 = (s32[128]{0:T(128)S(1)}, s32[128]{0:T(128)}, u32[]{:S(2)}) copy-start(s32[128]{0:T(128)} %param.16) | copy-start | bytes 1540
  1.4 0.9 %copy-start = (f32[8,32,128]{2,1,0:T(8,128)S(1)}, f32[8,32,128]{2,1,0:T(8,128)}, u32[]{:S(2)}) copy-start(f32[8,32,128]{2,1,0:T(8,128)} %charge_ref.1) | copy-start | bytes 393220
  2.3 0.9 %copy-start.1 = (f32[8,32,128]{2,1,0:T(8,128)S(1)}, f32[8,32,128]{2,1,0:T(8,128)}, u32[]{:S(2)}) copy-start(f32[8,32,128]{2,1,0:T(8,128)} %texture_ref.1) | copy-start | bytes 393220
  3.2 0.9 %copy-start.2 = (f32[8,32,128]{2,1,0:T(8,128)S(1)}, f32[8,32,128]{2,1,0:T(8,128)}, u32[]{:S(2)}) copy-start(f32[8,32,128]{2,1,0:T(8,128)} %initial_ref.1) | copy-start | bytes 393220
  4.1 0.8 %copy-start.3 = (f32[128,128]{1,0:T(8,128)S(1)}, f32[128,128]{1,0:T(8,128)}, u32[]{:S(2)}) copy-start(f32[128,128]{1,0:T(8,128)} %cond_ref.1) | copy-start | bytes 196612

commit v2 on v1

--- a/solution.py
+++ b/solution.py
@@ -15,7 +15,7 @@
 
 
 def each(low, high, body):
-    if high - low <= 16:
+    if high - low <= 32:
         for k in range(low, high):
             body(k)
     else:
@@ -25,6 +25,15 @@
         lax.fori_loop(low, high, step, 0)
 
 
+def middle_first(count, body):
+    half = count // 2
+    if count > 16:
+        each(1, count, body)
+        return
+    for k in sorted(range(1, count), key=lambda k: abs(k - half)):
+        body(k)
+
+
 def terms(value):
     high = value.astype(BF16).astype(F32)
     rest = value - high
@@ -34,6 +43,18 @@
 
 def kernel(
     sizes,
+    eps_in,
+    charge_in,
+    texture_in,
+    layer_in,
+    volts_in,
+    cond_in,
+    gate_in,
+    dest_in,
+    column_in,
+    initial_in,
+    out_ref,
+    norm_ref,
     eps_ref,
     charge_ref,
     texture_ref,
@@ -43,9 +64,9 @@
     gate_ref,
     dest_ref,
     column_ref,
-    initial_ref,
-    out_ref,
-    norm_ref,
+    load_sem,
+    rims,
+    faces_of,
     field,
     coef,
     blocks_out,
@@ -58,16 +79,12 @@
     coupled,
     part,
     sums,
-    part2,
-    sums2,
     block_send,
     block_recv,
     face_send,
     face_recv,
     sum_send,
     sum_recv,
-    sum2_send,
-    sum2_recv,
 ):
     grid_x, grid_y, grid_z, capacity, used = sizes
     peers = grid_x * grid_y
@@ -83,8 +100,13 @@
         target = lax.rem(me + k, peers)
         return target, {"gx": target // grid_y, "gy": lax.rem(target, grid_y)}
 
-    def layer(k):
-        return {"gz": lax.rem(iz + k, grid_z)}
+    devices = peers * grid_z
+    number = me * grid_z + iz
+
+    def anyone(k):
+        target = lax.rem(number + k, devices)
+        slab = target // grid_z
+        return {"gx": slab // grid_y, "gy": lax.rem(slab, grid_y), "gz": lax.rem(target, grid_z)}
 
     def beside(axis, side):
         return here[axis] > 0 if side == 0 else here[axis] < counts[axis] - 1
@@ -96,8 +118,23 @@
                 halo[:, side] = jnp.zeros(halo.shape[:1] + halo.shape[2:], F32)
 
     barrier = pltpu.get_barrier_semaphore()
-    each(1, peers, lambda k: pl.semaphore_signal(barrier, inc=1, device_id=peer(k)[1], device_id_type=MESH))
-    each(1, grid_z, lambda k: pl.semaphore_signal(barrier, inc=1, device_id=layer(k), device_id_type=MESH))
+    each(1, devices, lambda k: pl.semaphore_signal(barrier, inc=1, device_id=anyone(k), device_id_type=MESH))
+
+    pairs = (
+        (dest_in, dest_ref),
+        (column_in, column_ref),
+        (gate_in, gate_ref),
+        (volts_in, volts_ref),
+        (cond_in, cond_ref),
+        (eps_in, eps_ref),
+        (layer_in, layer_ref),
+        (texture_in, texture_ref),
+        (initial_in, field.at[1]),
+        (charge_in, charge_ref),
+    )
+    loads = [pltpu.make_async_copy(a, b, load_sem.at[i]) for i, (a, b) in enumerate(pairs)]
+    for load in loads:
+        load.start()
 
     lane = lax.broadcasted_iota(jnp.int32, (cy, cz), 1)
 
@@ -156,17 +193,8 @@
         high_z = jnp.where(lane3 == cz - 1, high_z, pltpu.roll(value, cz - 1, 2))
         return low_x, high_x, low_y, high_y, low_z, high_z
 
-    layers = layer_ref[...]
-    layer_eps = jnp.zeros(layers.shape, F32)
-    for m in range(eps_ref.shape[0]):
-        layer_eps = jnp.where(layers == m, eps_ref[m], layer_eps)
-    permittivity = texture_ref[...] * layer_eps[None]
-    field[0] = permittivity
-    pack(0, permittivity)
-    initial = initial_ref[...]
-    field[1] = initial
-    pack(1, initial)
-
+    for load in loads[:5]:
+        load.wait()
     count = cond_ref.shape[0]
     down = lax.broadcasted_iota(jnp.int32, (count, count), 0)
     across = lax.broadcasted_iota(jnp.int32, (count, count), 1)
@@ -206,7 +234,18 @@
     blocks_out[:, capacity + 2:, :] = jnp.zeros((peers, 6, cz), F32)
     each(0, peers, details)
 
-    pl.semaphore_wait(barrier, peers - 1 + grid_z - 1)
+    for load in loads[5:9]:
+        load.wait()
+    layers = layer_ref[...]
+    layer_eps = jnp.zeros(layers.shape, F32)
+    for m in range(eps_ref.shape[1]):
+        layer_eps = jnp.where(layers == m, eps_ref[:, m:m + 1], layer_eps)
+    permittivity = texture_ref[...] * layer_eps[None]
+    field[0] = permittivity
+    pack(0, permittivity)
+    pack(1, field[1])
+
+    pl.semaphore_wait(barrier, devices - 1)
 
     def block_copy(k):
         target, device = peer(k)
@@ -221,7 +260,7 @@
 
     send_faces(0)
     send_faces(1)
-    each(1, peers, lambda k: block_copy(k).start())
+    middle_first(peers, lambda k: block_copy(k).start())
 
     columns = cx * cy
     depth = -(-3 * capacity // cz) * cz
@@ -261,7 +300,8 @@
             total = total + coef[index] * pieces[index]
         return total
 
-    first = neighbours(1, initial_ref[...]) + charge_ref[...]
+    loads[9].wait()
+    first = neighbours(1, field[1]) + charge_ref[...]
     coef[6] = first
     coef[7] = diagonal
 
@@ -269,67 +309,83 @@
         block_copy(k).wait_recv()
         coupled[...] += product(blocks_in[k])
 
-    each(1, peers, arrive)
+    middle_first(peers, arrive)
     diagonal = coef[7] + coupled[:, :cz].reshape(cx, cy, cz)
     injected = coupled[:, cz:].reshape(cx, cy, cz)
     scale = RELAX / diagonal
-    potential = (1.0 - RELAX) * initial_ref[...] + scale * (coef[6] + injected)
+    potential = (1.0 - RELAX) * field[1] + scale * (coef[6] + injected)
     field[2] = potential
     pack(2, potential)
     send_faces(2)
-    for index in range(6):
-        coef[index] = coef[index] * scale
-    forcing = (charge_ref[...] + injected) * scale
-    coef[6] = forcing
+    scaled = [coef[index] * scale for index in range(6)]
+    coef[0] = scaled[0]
+    coef[1] = scaled[1]
+    coef[2] = jnp.where(row_y == 0, 0.0, scaled[2])
+    coef[3] = jnp.where(row_y == cy - 1, 0.0, scaled[3])
+    coef[4] = jnp.where(lane3 == 0, 0.0, scaled[4])
+    coef[5] = jnp.where(lane3 == cz - 1, 0.0, scaled[5])
+    faces_of[0] = scaled[2][:, 0, :]
+    faces_of[1] = scaled[3][:, cy - 1, :]
+    coef[8] = jnp.where(lane3 == 0, scaled[4], jnp.where(lane3 == cz - 1, scaled[5], 0.0))
+    coef[6] = (charge_ref[...] + injected) * scale
     coef[7] = diagonal * (1.0 / RELAX)
 
+    def inner(exchange):
+        value = field[exchange]
+        blank = jnp.zeros((1, cy, cz), F32)
+        total = coef[6] + coef[0] * jnp.concatenate([blank, value[:-1]], axis=0)
+        total = total + coef[1] * jnp.concatenate([value[1:], blank], axis=0)
+        total = total + coef[2] * pltpu.roll(value, 1, 1)
+        total = total + coef[3] * pltpu.roll(value, cy - 1, 1)
+        total = total + coef[4] * pltpu.roll(value, 1, 2)
+        return total + coef[5] * pltpu.roll(value, cz - 1, 2)
+
+    def outer(exchange):
+        rims[0] += coef[0, 0] * halo_x[exchange, 0]
+        rims[cx - 1] += coef[1, cx - 1] * halo_x[exchange, 1]
+        low_y = (faces_of[0] * halo_y[exchange, 0])[:, None, :]
+        high_y = (faces_of[1] * halo_y[exchange, 1])[:, None, :]
+        low_face, high_face = halo_z[exchange, 0], halo_z[exchange, 1]
+        near = []
+        for x in range(cx):
+            near.append(jnp.where(lane < cz // 2, low_face[:, x:x + 1], high_face[:, cx + x:cx + x + 1]))
+        total = rims[...] + jnp.where(row_y == 0, low_y, 0.0) + jnp.where(row_y == cy - 1, high_y, 0.0)
+        return total + coef[8] * jnp.stack(near)
+
     for exchange in range(2, exchanges - 1):
+        rims[...] = inner(exchange) + (1.0 - RELAX) * field[exchange]
         wait_faces(exchange)
-        potential = field[exchange]
-        potential = (1.0 - RELAX) * potential + (coef[6] + neighbours(exchange, potential))
+        potential = outer(exchange)
         field[exchange + 1] = potential
         pack(exchange + 1, potential)
         send_faces(exchange + 1)
 
     last = exchanges - 1
-    out_ref[...] = field[last]
+    store = pltpu.make_async_copy(field.at[last], out_ref, load_sem.at[0])
+    store.start()
+    rims[...] = inner(last) - RELAX * field[last]
     wait_faces(last)
-    potential = field[last]
-    residual = (coef[6] + neighbours(last, potential) - RELAX * potential) * coef[7]
+    residual = outer(last) * coef[7]
     squares = jnp.sum(residual * residual, axis=0)
     total = squares[:8]
     for y in range(8, cy, 8):
         total = total + squares[y:y + 8]
 
+    total = jnp.sum(total, axis=0, keepdims=True)
     part[...] = total
-    sums[me] = total
+    sums[number] = total
 
     def sum_copy(k):
         return pltpu.make_async_remote_copy(
             src_ref=part,
-            dst_ref=sums.at[me],
+            dst_ref=sums.at[number],
             send_sem=sum_send.at[k],
             recv_sem=sum_recv.at[k],
-            device_id=peer(k)[1],
+            device_id=anyone(k),
             device_id_type=MESH,
         )
 
-    def sum2_copy(k):
-        return pltpu.make_async_remote_copy(
-            src_ref=part2,
-            dst_ref=sums2.at[iz],
-            send_sem=sum2_send.at[k],
-            recv_sem=sum2_recv.at[k],
-            device_id=layer(k),
-            device_id_type=MESH,
-        )
-
-    each(1, peers, lambda k: sum_copy(k).start())
-    each(1, peers, lambda k: sum_copy(k).wait_recv())
-    total = jnp.sum(sums[...], axis=0)
-    part2[...] = total
-    sums2[iz] = total
-    each(1, grid_z, lambda k: sum2_copy(k).start())
+    each(1, devices, lambda k: sum_copy(k).start())
     each(1, peers, lambda k: block_copy(k).wait_send())
     for exchange in range(exchanges):
         for axis in range(3):
@@ -337,12 +393,12 @@
                 @pl.when(beside(axis, side))
                 def _(exchange=exchange, axis=axis, side=side):
                     face_copy(exchange, axis, side).wait_send()
-    each(1, peers, lambda k: sum_copy(k).wait_send())
-    each(1, grid_z, lambda k: sum2_copy(k).wait_recv())
-    total = jnp.sum(sums2[...], axis=0)
-    cells = cx * cy * cz * grid_x * grid_y * grid_z
+    each(1, devices, lambda k: sum_copy(k).wait_send())
+    each(1, devices, lambda k: sum_copy(k).wait_recv())
+    total = jnp.sum(sums[...], axis=0)
+    cells = cx * cy * cz * devices
+    store.wait()
     norm_ref[...] = jnp.sqrt(jnp.sum(total, keepdims=True) / cells)
-    each(1, grid_z, lambda k: sum2_copy(k).wait_send())
 
 
 def on_device(
@@ -367,11 +423,23 @@
     potential, norm = pl.pallas_call(
         functools.partial(kernel, sizes),
         out_shape=(jax.ShapeDtypeStruct(charge.shape, F32), jax.ShapeDtypeStruct((1, 1), F32)),
-        in_specs=[pl.BlockSpec(memory_space=pltpu.SMEM)] + [vmem] * 9,
-        out_specs=(vmem, vmem),
+        in_specs=[pl.BlockSpec(memory_space=pltpu.HBM)] * 10,
+        out_specs=(pl.BlockSpec(memory_space=pltpu.HBM), vmem),
         scratch_shapes=[
+            pltpu.VMEM((1, material_eps.shape[0]), F32),
+            pltpu.VMEM((cx, cy, cz), F32),
+            pltpu.VMEM((cx, cy, cz), F32),
+            pltpu.VMEM((1, cz), jnp.int32),
+            pltpu.VMEM((1, gate_volts.shape[0]), F32),
+            pltpu.VMEM(block_cond.shape, F32),
+            pltpu.VMEM((1, block_gate.shape[0]), jnp.int32),
+            pltpu.VMEM((1, block_dest.shape[0]), jnp.int32),
+            pltpu.VMEM((1, block_column.shape[0]), jnp.int32),
+            dma((10,)),
+            pltpu.VMEM((cx, cy, cz), F32),
+            pltpu.VMEM((2, cx, cz), F32),
             pltpu.VMEM((exchanges, cx, cy, cz), F32),
-            pltpu.VMEM((8, cx, cy, cz), F32),
+            pltpu.VMEM((9, cx, cy, cz), F32),
             pltpu.VMEM((peers, capacity + 8, cz), F32),
             pltpu.VMEM((peers, capacity + 8, cz), F32),
             pltpu.VMEM((exchanges, 2, cx, cz), F32),
@@ -380,24 +448,20 @@
             pltpu.VMEM((exchanges, 2, cx, cz), F32),
             pltpu.VMEM((exchanges, 2, cy, cz), F32),
             pltpu.VMEM((cx * cy, 2 * cz), F32),
-            pltpu.VMEM((8, cz), F32),
-            pltpu.VMEM((peers, 8, cz), F32),
-            pltpu.VMEM((8, cz), F32),
-            pltpu.VMEM((grid_z, 8, cz), F32),
+            pltpu.VMEM((1, cz), F32),
+            pltpu.VMEM((peers * grid_z, 1, cz), F32),
             dma((peers,)),
             dma((peers,)),
             dma((exchanges, 6)),
             dma((exchanges, 6)),
-            dma((peers,)),
-            dma((peers,)),
-            dma((grid_z,)),
-            dma((grid_z,)),
+            dma((peers * grid_z,)),
+            dma((peers * grid_z,)),
         ],
         compiler_params=pltpu.CompilerParams(
-            collective_id=0, has_side_effects=True, vmem_limit_bytes=32 * 1024 * 1024
+            collective_id=0, has_side_effects=True, vmem_limit_bytes=60 * 1024 * 1024
         ),
     )(
-        material_eps,
+        material_eps[None, :],
         charge,
         texture,
         layer_material[None, :],

time: 45.7 us -> 40.5 us (0.89)
  local copies, waits for them, and re-layouts: 4.89 us -> 1.57 us
  Pallas kernels: 38.1 us -> 36.3 us
    unnamed x21 -> x1, local copies, waits for them, and re-layouts: 4.89 us -> 1.57 us
    pallas_call x1, Pallas kernels: 38.1 us -> 36.3 us  [on_device(): pl.pallas_call(functools.partial(kernel, sizes), out_shape=(jax.ShapeDtyp...]
where the time goes in v2:
time: 40.5 us; the launch traced here: 40.4 us
  Pallas kernels  36.3 us (90%)
  between operations  2.45 us (6%)
  local copies, waits for them, and re-layouts  1.57 us (4%)
    pallas_call x1, Pallas kernels, on_device(): pl.pallas_call(functools.partial(kernel, sizes), out_shape=(jax.ShapeDtyp...  36.3 us
    unnamed x1, local copies, waits for them, and re-layouts  1.57 us

profile of v2, /device:TPU:0, one launch (start us, length us, event | category | flops | bytes accessed | tf_op | source)
XLA Modules:
  0.0 40.4 jit_solution(6975635323863437199)
XLA Ops:
  0.6 36.3 %shard_map.113 = (f32[8,32,128]{2,1,0:T(8,128)}, f32[1,1]{1,0:T(1,128)}) custom-call(f32[1,6]{1,0:T(1,128)} %bitcast.8, f32[8,32,128]{2,1,0:T(8,128)} %charge_in.1, f32[8,32,128]{2,1,0:T(8,128)} %texture_in.1, s32[1,128]{1,0:T(1,128)} %bitcast.9, f32[1,1000]{1,0:T(1,128)} %bitcast.7, f32[128,128]{1,0:T(8,128)} %cond_in.1, s32[1,128]{1,0:T(1,128)} %bitcast.10, ...), custom_call_target="tpu_custom_call" | custom-call | tf_op jit(solution)/shard_map/pallas_call | solution.py:423
  37.0 1.6 %copy.14 = f32[8,32,128]{2,1,0:T(8,128)} copy(f32[8,32,128]{2,1,0:T(8,128)} %get-tuple-element.8) | data formatting | bytes 262144

commit v3 on v2

--- a/solution.py
+++ b/solution.py
@@ -27,7 +27,7 @@
 
 def middle_first(count, body):
     half = count // 2
-    if count > 16:
+    if count > 32:
         each(1, count, body)
         return
     for k in sorted(range(1, count), key=lambda k: abs(k - half)):
@@ -136,28 +136,40 @@
     for load in loads:
         load.start()
 
-    lane = lax.broadcasted_iota(jnp.int32, (cy, cz), 1)
+    lane8 = lax.broadcasted_iota(jnp.int32, (8, cz), 1)
+    half = cx * cy // 8
+
+    def spread(face, x, start):
+        tiles = []
+        for b in range(cy // 8):
+            j = start + x + cx * b
+            tiles.append(jnp.broadcast_to(face[:, j:j + 1], (8, cz)))
+        return jnp.concatenate(tiles, axis=0)
 
     def pack(exchange, value):
         face_y[exchange, 0] = value[:, 0, :]
         face_y[exchange, 1] = value[:, cy - 1, :]
-        faces = jnp.zeros((cy, cz), F32)
+        top = jnp.zeros((8, cz), F32)
+        bottom = jnp.zeros((8, cz), F32)
         for x in range(cx):
-            faces = jnp.where(lane == x, value[x, :, cz - 1:cz], faces)
-            faces = jnp.where(lane == cx + x, value[x, :, 0:1], faces)
-        face_z[exchange] = faces
+            for b in range(cy // 8):
+                rows = value[x, 8 * b:8 * b + 8]
+                top = jnp.where(lane8 == x + cx * b, rows[:, cz - 1:cz], top)
+                bottom = jnp.where(lane8 == half + x + cx * b, rows[:, 0:1], bottom)
+        face_z[exchange] = jnp.where(lane8 < half, top, bottom)
 
     def face_copy(exchange, axis, side):
         step = counts[axis] - 1 if side == 0 else 1
+        at = pl.ds(0, 2) if exchange == 0 else exchange
         if axis == 0:
-            source, target = field.at[exchange, 0 if side == 0 else cx - 1], halo_x
+            source, target = field.at[at, 0 if side == 0 else cx - 1], halo_x
         elif axis == 1:
-            source, target = face_y.at[exchange, side], halo_y
+            source, target = face_y.at[at, side], halo_y
         else:
-            source, target = face_z.at[exchange], halo_z
+            source, target = face_z.at[at], halo_z
         return pltpu.make_async_remote_copy(
             src_ref=source,
-            dst_ref=target.at[exchange, 1 - side],
+            dst_ref=target.at[at, 1 - side],
             send_sem=face_send.at[exchange, 2 * axis + side],
             recv_sem=face_recv.at[exchange, 2 * axis + 1 - side],
             device_id={names[axis]: lax.rem(here[axis] + step, counts[axis])},
@@ -187,8 +199,8 @@
         low_y = jnp.where(row_y == 0, halo_y[exchange, 0][:, None, :], pltpu.roll(value, 1, 1))
         high_y = jnp.where(row_y == cy - 1, halo_y[exchange, 1][:, None, :], pltpu.roll(value, cy - 1, 1))
         low_face, high_face = halo_z[exchange, 0], halo_z[exchange, 1]
-        low_z = jnp.stack([jnp.broadcast_to(low_face[:, x:x + 1], (cy, cz)) for x in range(cx)])
-        high_z = jnp.stack([jnp.broadcast_to(high_face[:, cx + x:cx + x + 1], (cy, cz)) for x in range(cx)])
+        low_z = jnp.stack([spread(low_face, x, 0) for x in range(cx)])
+        high_z = jnp.stack([spread(high_face, x, half) for x in range(cx)])
         low_z = jnp.where(lane3 == 0, low_z, pltpu.roll(value, 1, 2))
         high_z = jnp.where(lane3 == cz - 1, high_z, pltpu.roll(value, cz - 1, 2))
         return low_x, high_x, low_y, high_y, low_z, high_z
@@ -259,7 +271,6 @@
         )
 
     send_faces(0)
-    send_faces(1)
     middle_first(peers, lambda k: block_copy(k).start())
 
     columns = cx * cy
@@ -291,7 +302,6 @@
         diagonal = diagonal + coefficients[index]
     for index in range(6):
         coef[index] = coefficients[index]
-    wait_faces(1)
 
     def neighbours(exchange, value):
         pieces = shifted(exchange, value)
@@ -348,7 +358,7 @@
         low_face, high_face = halo_z[exchange, 0], halo_z[exchange, 1]
         near = []
         for x in range(cx):
-            near.append(jnp.where(lane < cz // 2, low_face[:, x:x + 1], high_face[:, cx + x:cx + x + 1]))
+            near.append(jnp.where(lane3[0] < cz // 2, spread(low_face, x, 0), spread(high_face, x, half)))
         total = rims[...] + jnp.where(row_y == 0, low_y, 0.0) + jnp.where(row_y == cy - 1, high_y, 0.0)
         return total + coef[8] * jnp.stack(near)
 
@@ -385,9 +395,9 @@
             device_id_type=MESH,
         )
 
-    each(1, devices, lambda k: sum_copy(k).start())
+    middle_first(devices, lambda k: sum_copy(k).start())
     each(1, peers, lambda k: block_copy(k).wait_send())
-    for exchange in range(exchanges):
+    for exchange in (0, *range(2, exchanges)):
         for axis in range(3):
             for side in range(2):
                 @pl.when(beside(axis, side))
@@ -443,10 +453,10 @@
             pltpu.VMEM((peers, capacity + 8, cz), F32),
             pltpu.VMEM((peers, capacity + 8, cz), F32),
             pltpu.VMEM((exchanges, 2, cx, cz), F32),
-            pltpu.VMEM((exchanges, cy, cz), F32),
+            pltpu.VMEM((exchanges, 8, cz), F32),
             pltpu.VMEM((exchanges, 2, cy, cz), F32),
             pltpu.VMEM((exchanges, 2, cx, cz), F32),
-            pltpu.VMEM((exchanges, 2, cy, cz), F32),
+            pltpu.VMEM((exchanges, 2, 8, cz), F32),
             pltpu.VMEM((cx * cy, 2 * cz), F32),
             pltpu.VMEM((1, cz), F32),
             pltpu.VMEM((peers * grid_z, 1, cz), F32),

time: 40.5 us -> 39.9 us (0.985)
  Pallas kernels: 36.3 us -> 35.7 us
    pallas_call x1, Pallas kernels: 36.3 us -> 35.7 us  [on_device(): pl.pallas_call(functools.partial(kernel, sizes), out_shape=(jax.ShapeDtyp...]
where the time goes in v3:
time: 39.9 us; the launch traced here: 39.7 us
  Pallas kernels  35.7 us (89%)
  between operations  2.45 us (6%)
  local copies, waits for them, and re-layouts  1.57 us (4%)
    pallas_call x1, Pallas kernels, on_device(): pl.pallas_call(functools.partial(kernel, sizes), out_shape=(jax.ShapeDtyp...  35.7 us
    unnamed x1, local copies, waits for them, and re-layouts  1.57 us

profile of v3, /device:TPU:0, one launch (start us, length us, event | category | flops | bytes accessed | tf_op | source)
XLA Modules:
  0.0 39.7 jit_solution(18134524283768502731)
XLA Ops:
  0.6 35.7 %shard_map.113 = (f32[8,32,128]{2,1,0:T(8,128)}, f32[1,1]{1,0:T(1,128)}) custom-call(f32[1,6]{1,0:T(1,128)} %bitcast.8, f32[8,32,128]{2,1,0:T(8,128)} %charge_in.1, f32[8,32,128]{2,1,0:T(8,128)} %texture_in.1, s32[1,128]{1,0:T(1,128)} %bitcast.9, f32[1,1000]{1,0:T(1,128)} %bitcast.7, f32[128,128]{1,0:T(8,128)} %cond_in.1, s32[1,128]{1,0:T(1,128)} %bitcast.10, ...), custom_call_target="tpu_custom_call" | custom-call | tf_op jit(solution)/shard_map/pallas_call | solution.py:433
  36.3 1.6 %copy.14 = f32[8,32,128]{2,1,0:T(8,128)} copy(f32[8,32,128]{2,1,0:T(8,128)} %get-tuple-element.8) | data formatting | bytes 262144
